TPU v7x, 32 devices: a whole 2x2x4 slice. The times are simulated.
32 devices in a mesh: parts: 2 (over x), tm: 2 (over core), node: 8 (over z, y).
Axes of the slice: x: 2, y: 2, z: 4, core: 2. Of those that a mesh axis runs over, the one named last changes fastest.
Arguments:
- initial_fields: float32 [4, 32768], P('parts', 'node'), parts along dimension 0, may hold values from 0 to 1
- feed_rate: float32 [32768], P('node'), may hold values from 0.05 to 0.5
- kill_rate: float32 [32768], P('node'), may hold values from 0.05 to 1
- fine_tiles: float32 [256, 3, 128, 128], P('node'), may hold values from -0.3125 to 0.3125
- fine_cols: int32 [256, 3], P('node'), may hold values from 0 to 55, as said below
- fine_halo: int32 [24576], P('node'), may hold values from 0 to 4095, as said below
- coarse_tiles: float32 [64, 3, 128, 128], P('node'), may hold values from -0.3125 to 0.3125
- coarse_cols: int32 [64, 3], P('node'), may hold values from 0 to 13, as said below
- coarse_halo: int32 [6144], P('node'), may hold values from 0 to 1023, as said below
- children: int32 [32768], P('node'), may hold values from 0 to 4095, as said below
Outputs:
- final_states: float32 [8, 4, 32768], P('tm', 'parts', 'node'), parts along dimension 1
There are 2 independent parts, one for each index of `parts`. A program takes and returns all parts, laid end to end along the dimension named above; an argument that names none is the same for every part. Nothing has to cross between parts.
Inputs may be any that keep to these rules, and one draw needn't show every extreme that they name: `fine_cols`: entry 0 of row block r of a band is 12 + r, its own block; the others lie within 12 blocks of it. Blocks are counted over the extended rows: 12 halo blocks from the band below, the band's 32 own blocks, then 12 halo blocks from the band above. The lowest band names no block under 12, the highest none at 44 or above. `coarse_cols`: entry 0 of coarse row block r of a band is 3 + r; the others lie within 3 blocks of it, counted as for fine_cols with 3 halo blocks on each side and 8 own blocks. The lowest band names no block under 3, the highest none at 11 or above. `fine_halo`: each band has 3072 entries, rows of that band: the first 1536 are distinct rows under 2 * 1536, row 0 among them; the last 1536 are distinct rows at 1024 or above, the band's last row among them. `coarse_halo`: each band has 768 entries, coarse rows of that band: the first 384 are distinct rows under 2 * 384, row 0 among them; the last 384 are distinct rows at 256 or above, the band's last row among them. `children`: the 4096 entries of each band are a permutation of its rows 0 to 4095.
All inputs are finite; a program needn't handle non-finite values.
Results may differ from a plain program's by a relative error of at most 0.0001.
Values sent between devices are 32-bit elements; how exact they have to be, the bound alone decides.
A program may use at most 128 MiB of HBM per device.

v0:
```python
import jax
import jax.numpy as jnp
from jax import lax
from jax.sharding import PartitionSpec as P

TS_DEV = 4
ITERS = 2


highest = lax.Precision.HIGHEST
diffusion_u = 1.0
diffusion_v = 0.5
self_weight = 1.5
slice_step = 0.25
half_step = 0.125
quad_rows = ((5.0 / 24.0, 1.0 / 3.0, -1.0 / 24.0), (-1.0 / 24.0, 1.0 / 3.0, 5.0 / 24.0))


def with_halo(block, sides, width):
    for axis, dim in sides:
        count = lax.axis_size(axis)
        forward = [(i, i + 1) for i in range(count - 1)]
        backward = [(target, source) for source, target in forward]
        low = lax.ppermute(
            lax.slice_in_dim(block, block.shape[dim] - width, None, axis=dim), axis, forward
        )
        high = lax.ppermute(lax.slice_in_dim(block, 0, width, axis=dim), axis, backward)
        block = jnp.concatenate([low, block, high], axis=dim)
    return block


def from_behind(block, axis, distance):
    devices = range(lax.axis_size(axis))
    route = [(i - distance, i) for i in devices if i - distance in devices]
    return lax.ppermute(block, axis, route)


def stencil_product(flattened, padded, rim_width, tiles, columns):
    tile_size = tiles.shape[-1]
    extended = jnp.concatenate(
        [padded[:, :rim_width], flattened, padded[:, 3 * rim_width :]], axis=1
    )
    extended = extended.reshape((flattened.shape[0], -1, tile_size))
    picked = extended[:, columns]
    combined = jnp.einsum("bsij,cbsj->cbi", tiles, picked, precision=highest)
    return combined.reshape(flattened.shape) - self_weight * flattened


def fine_operator(field, tiles, columns, rim_rows):
    flattened = field.reshape((-1, field.shape[-1]))
    rim_width = rim_rows.shape[0] // 2
    padded = with_halo(flattened[:, rim_rows], (("node", 1),), rim_width)
    return stencil_product(flattened, padded, rim_width, tiles, columns).reshape(field.shape)


def coarse_operator(field, tiles, columns, rim_rows):
    flattened = field.reshape((-1, field.shape[-1]))
    rim_width = rim_rows.shape[0] // 2
    padded = with_halo(flattened[:, rim_rows], (("node", 1),), rim_width)
    return stencil_product(flattened, padded, rim_width, tiles, columns).reshape(field.shape)


def transfer_matrix(children):
    fine_count = children.shape[0]
    coarse_count = fine_count // 4
    position = (
        jnp.zeros((fine_count,), jnp.int32)
        .at[children]
        .set(jnp.arange(fine_count, dtype=jnp.int32))
    )
    owner = position // 4
    return jnp.where(
        owner[:, None] == jnp.arange(coarse_count, dtype=jnp.int32)[None, :], 0.25, 0.0
    ).astype(jnp.float32)


def restrict(field, mapping):
    flattened = field.reshape((-1, field.shape[-1]))
    summed = jnp.dot(flattened, mapping, precision=highest, preferred_element_type=jnp.float32)
    return summed.reshape(field.shape[:-1] + (-1,))


def prolong(coarse, mapping):
    flattened = coarse.reshape((-1, coarse.shape[-1]))
    placed = jnp.einsum("rc,fc->rf", flattened, mapping, precision=highest) * 4.0
    return placed.reshape(coarse.shape[:-1] + (-1,))


def explicit(state, laplacian, source):
    growth = state[..., 0, :] * state[..., 1, :] * state[..., 1, :]
    first_row = diffusion_u * laplacian[..., 0, :] - growth + source
    second_row = diffusion_v * laplacian[..., 1, :] + growth
    return jnp.stack([first_row, second_row], axis=-2)


def advance(previous, terms_new, terms_old, old_next, decay, integral, defect):
    return (
        previous
        + half_step * (terms_new - terms_old)
        + half_step * decay * old_next
        + integral
        + defect
    ) / (1.0 + half_step * decay)


def quadrature(values):
    pieces = []
    for weights in quad_rows:
        pieces.append(
            slice_step
            * (
                weights[0] * values[..., 0, :, :]
                + weights[1] * values[..., 1, :, :]
                + weights[2] * values[..., 2, :, :]
            )
        )
    return jnp.stack(pieces, axis=-3)


def run_chain(
    first_value, coarse_nodes, coarse_values, coarse_quad, defects, coarse_terms, coarse_decay
):
    is_first = lax.axis_index("tm") == 0

    def advance_slice(current, inputs):
        node_values, term_values, quad_values, defect = inputs
        node_one = advance(
            current,
            coarse_terms(current),
            term_values[0],
            node_values[1],
            coarse_decay,
            quad_values[0],
            defect[0],
        )
        node_two = advance(
            node_one,
            coarse_terms(node_one),
            term_values[1],
            node_values[2],
            coarse_decay,
            quad_values[1],
            defect[1],
        )
        return (node_two, jnp.stack([node_one, node_two]))

    incoming = first_value
    results = None
    section_count = lax.axis_size("tm")
    for section_index in range(section_count):
        initial = jnp.where(is_first, first_value, incoming)
        final_state, results = lax.scan(
            advance_slice, initial, (coarse_nodes, coarse_values, coarse_quad, defects)
        )
        if section_index + 1 < section_count:
            incoming = from_behind(final_state, "tm", 1)
    return results


def per_device(
    initial_fields,
    feed_rate,
    kill_rate,
    fine_tiles,
    fine_cols,
    fine_halo,
    coarse_tiles,
    coarse_cols,
    coarse_halo,
    children,
):
    mapping = transfer_matrix(children)
    decay = jnp.stack([feed_rate, feed_rate + kill_rate])
    coarse_decay = restrict(decay, mapping)
    is_first = lax.axis_index("tm") == 0

    def fine_terms(state):
        return explicit(state, fine_operator(state, fine_tiles, fine_cols, fine_halo), feed_rate)

    def coarse_terms(state):
        return explicit(
            state, coarse_operator(state, coarse_tiles, coarse_cols, coarse_halo), coarse_decay[0]
        )

    base = restrict(initial_fields, mapping)
    base_terms = coarse_terms(base)
    base_values = base_terms - coarse_decay * base
    base_quad = quadrature(jnp.stack([base_values, base_values, base_values]))
    node_shape = (TS_DEV, 3) + base.shape
    results = run_chain(
        base,
        jnp.broadcast_to(base, node_shape),
        jnp.broadcast_to(base_terms, node_shape),
        jnp.broadcast_to(base_quad, (TS_DEV, 2) + base.shape),
        jnp.zeros((TS_DEV, 2) + base.shape, jnp.float32),
        coarse_terms,
        coarse_decay,
    )
    states = initial_fields + prolong(results - base, mapping)
    for iteration in range(ITERS):
        received = from_behind(states[-1, 1], "tm", 1)
        start_state = jnp.where(is_first, initial_fields, received)
        pair_terms = fine_terms(states)
        start_terms = fine_terms(start_state[None])[0]
        start_nodes = jnp.concatenate([start_state[None], states[:-1, 1]], axis=0)
        start_values = jnp.concatenate([start_terms[None], pair_terms[:-1, 1]], axis=0)
        node_values = jnp.stack([start_nodes, states[:, 0], states[:, 1]], axis=1)
        term_values = jnp.stack([start_values, pair_terms[:, 0], pair_terms[:, 1]], axis=1)
        node_values, term_values = (node_values, term_values)
        fine_quad = quadrature(term_values - decay * node_values)
        node_one = advance(
            node_values[:, 0],
            term_values[:, 0],
            term_values[:, 0],
            node_values[:, 1],
            decay,
            fine_quad[:, 0],
            0.0,
        )
        terms_one = fine_terms(node_one)
        node_two = advance(
            node_one, terms_one, term_values[:, 1], node_values[:, 2], decay, fine_quad[:, 1], 0.0
        )
        terms_two = fine_terms(node_two)
        swept = jnp.stack([node_values[:, 0], node_one, node_two], axis=1)
        swept_terms = jnp.stack([term_values[:, 0], terms_one, terms_two], axis=1)
        coarse_nodes = restrict(swept, mapping)
        coarse_values = coarse_terms(coarse_nodes)
        coarse_parts = coarse_values - coarse_decay * coarse_nodes
        coarse_quad = quadrature(coarse_parts)
        defects = quadrature(restrict(swept_terms - decay * swept, mapping) - coarse_parts)
        results = run_chain(
            coarse_nodes[0, 0],
            coarse_nodes,
            coarse_values,
            coarse_quad,
            defects,
            coarse_terms,
            coarse_decay,
        )
        states = swept[:, 1:] + prolong(results - coarse_nodes[:, 1:], mapping)
    return states[:, 1]


def solution(mesh):
    return jax.shard_map(
        per_device,
        mesh=mesh,
        in_specs=(
            P("parts", "node"),
            P("node"),
            P("node"),
            P("node", None, None, None),
            P("node", None),
            P("node"),
            P("node", None, None, None),
            P("node", None),
            P("node"),
            P("node"),
        ),
        out_specs=P("tm", "parts", "node"),
        check_vma=False,
    )
```

profile of v0, /device:TPU:1, one launch (start us, length us, event | category | flops | bytes accessed | tf_op | source)
XLA Modules:
  0.0 1422.5 jit_solution(14744903833291985754)
XLA Ops:
  0.7 15.5 %scatter_custom_fusion = s32[4096]{0:T(1024)S(1)} fusion(s32[4096]{0:T(1024)S(1)} %compare_select_fusion.12, s32[4096]{0:T(1024)S(1)} %iota.7, s32[]{:T(128)} %constant.140.clone.1), kind=kCustom, calls=%fused_computation.609 | custom fusion | bytes 16388 | tf_op jit(solution)/shard_map/scatter | solution.py:69
  16.3 33.1 %fusion.192 = f32[2,1024]{1,0:T(2,128)S(1)} fusion(f32[2,4096]{1,0:T(2,128)} %param.22, s32[4096]{0:T(1024)S(1)} %add_select_fusion), kind=kOutput, calls=%fused_computation.377 | convolution fusion | flops 109051904 | bytes 57344 | tf_op jit(solution)/shard_map/dot_general | solution.py:79
  70.0 146.5 %while.66 = (s32[]{:T(128)}, f32[2,1024]{1,0:T(2,128)S(1)}, s32[768]{0:T(1024)S(1)}, s32[8,3]{0,1:T(4,128)S(1)}, f32[8,3,128,128]{3,2,1,0:T(8,128)S(1)}, /*index...) while((s32[]{:T(128)}, f32[2,1024]{1,0:T(2,128)S(1)}, ...), condition=%wide.region_2.3_spmd, body=%wide.region_1.2_spmd.sunk | while | flops 18954572 | bytes 3735729 | solution.py:152
  220.2 154.4 %while.67 = (s32[]{:T(128)}, f32[2,1024]{1,0:T(2,128)S(1)}, f32[4,2,2,1024]{3,2,1,0:T(2,128)}, s32[768]{0:T(1024)S(1)}, s32[8,3]{0,1:T(4,128)S(1)}, /*index=5*/f...) while((s32[]{:T(128)}, f32[2,1024]{1,0:T(2,128)S(1)}, ...), condition=%wide.region_4.5_spmd, body=%wide.region_3.4_spmd.sunk | while | flops 18958668 | bytes 3768509 | solution.py:152
  375.5 16.0 %fusion.325 = (f32[16,4096]{1,0:T(8,128)S(1)}, f32[16,4096]{1,0:T(8,128)S(1)}) fusion(f32[16,4096]{1,0:T(8,128)} %add.923, f32[16,1024]{1,0:T(8,128)S(1)} %reshape.846, s32[4096]{0:T(1024)S(1)} %add_select_fusion), kind=kOutput, calls=%fused_computation.676 | convolution fusion | flops 813826048 | bytes 868352 | tf_op jit(solution)/shard_map/rc,fc->rf/dot_general | solution.py:85
  395.7 12.7 gather_fusion.28
  413.0 12.5 gather_fusion.26
  466.5 12.5 gather_fusion.30
  513.5 12.5 gather_fusion.34
  553.7 9.5 fusion.143
  576.9 11.6 fusion.189
  589.9 128.0 %while.68 = (s32[]{:T(128)}, f32[2,1024]{1,0:T(2,128)S(1)}, s32[768]{0:T(1024)S(1)}, s32[8,3]{0,1:T(4,128)S(1)}, f32[8,3,128,128]{3,2,1,0:T(8,128)S(1)}, /*index...) while((s32[]{:T(128)}, f32[2,1024]{1,0:T(2,128)S(1)}, ...), condition=%wide.region_6.7_spmd, body=%wide.region_5.6_spmd.sunk | while | flops 18958668 | bytes 3752121 | solution.py:152
  721.1 14.9 %collective-permute-done.38 = f32[2,1024]{1,0:T(2,128)S(1)} collective-permute-done((f32[2,1024]{1,0:T(2,128)S(1)}, f32[2,1024]{1,0:T(2,128)S(1)}, u32[]{:S(2)}, u32[]{:S(2)}) %collective-permute-start.38) | collective-permute-done | bytes 8224 | tf_op jit(solution)/shard_map/ppermute | solution.py:35
  736.7 154.6 %while.69 = (s32[]{:T(128)}, f32[2,1024]{1,0:T(2,128)S(1)}, f32[4,2,2,1024]{3,2,1,0:T(2,128)}, s32[768]{0:T(1024)S(1)}, s32[8,3]{0,1:T(4,128)S(1)}, /*index=5*/f...) while((s32[]{:T(128)}, f32[2,1024]{1,0:T(2,128)S(1)}, ...), condition=%wide.region_8.9_spmd, body=%wide.region_7.8_spmd.sunk | while | flops 18962764 | bytes 3784901 | solution.py:152
  892.2 16.0 %fusion.326 = (f32[16,4096]{1,0:T(8,128)S(1)}, f32[16,4096]{1,0:T(8,128)S(1)}) fusion(f32[16,4096]{1,0:T(8,128)} %stack.292, f32[16,1024]{1,0:T(8,128)S(1)} %reshape.863, s32[4096]{0:T(1024)S(1)} %copy-done.90), kind=kOutput, calls=%fused_computation.677 | convolution fusion | flops 813826048 | bytes 868352 | tf_op jit(solution)/shard_map/rc,fc->rf/dot_general | solution.py:85
  910.2 12.5 gather_fusion.38
  951.4 12.5 gather_fusion.36
  989.8 12.5 gather_fusion.40
  1036.9 12.5 gather_fusion.44
  1098.2 11.4 fusion.190
  1109.7 125.9 %while.70 = (s32[]{:T(128)}, f32[2,1024]{1,0:T(2,128)S(1)}, s32[768]{0:T(1024)S(1)}, s32[8,3]{0,1:T(4,128)S(1)}, f32[8,3,128,128]{3,2,1,0:T(8,128)S(1)}, /*index...) while((s32[]{:T(128)}, f32[2,1024]{1,0:T(2,128)S(1)}, ...), condition=%wide.region_10.11_spmd, body=%wide.region_9.10_spmd.sunk | while | flops 18958668 | bytes 3752121 | solution.py:152
  1237.8 16.0 %collective-permute-done.50 = f32[2,1024]{1,0:T(2,128)S(1)} collective-permute-done((f32[2,1024]{1,0:T(2,128)S(1)}, f32[2,1024]{1,0:T(2,128)S(1)}, u32[]{:S(2)}, u32[]{:S(2)}) %collective-permute-start.50) | collective-permute-done | bytes 8224 | tf_op jit(solution)/shard_map/ppermute | solution.py:35
  1253.8 152.1 %while.71 = (s32[]{:T(128)}, f32[2,1024]{1,0:T(2,128)S(1)}, f32[4,2,2,1024]{3,2,1,0:T(2,128)S(1)}, s32[768]{0:T(1024)S(1)}, s32[8,3]{0,1:T(4,128)S(1)}, /*index=...) while((s32[]{:T(128)}, f32[2,1024]{1,0:T(2,128)S(1)}, ...), condition=%wide.region_12.13_spmd, body=%wide.region_11.12_spmd.sunk | while | flops 18962764 | bytes 3784901 | solution.py:152
  1406.0 15.1 %fusion.186 = f32[16,4096]{1,0:T(8,128)S(1)} fusion(f32[16,1024]{1,0:T(8,128)S(1)} %reshape.879, s32[4096]{0:T(1024)S(1)} %copy-done.91), kind=kOutput, calls=%fused_computation.362 | convolution fusion | flops 813760512 | bytes 344064 | tf_op jit(solution)/shard_map/rc,fc->rf/dot_general | solution.py:85
  (1299 shorter events, 1156.5 us)
Async XLA Ops:
  51.4 15.4 %collective-permute-start.24 = (f32[2,384]{1,0:T(2,128)S(1)}, f32[2,384]{1,0:T(2,128)S(1)}, u32[]{:S(2)}, u32[]{:S(2)}) collective-permute-start(f32[2,384]{1,0:T(2,128)S(1)} %get-tuple-element.1150), channel_id=1, source_target_pairs={{0,1},{1,2},{2,3},{3,4},{4,5},{5,6},{6,7},{8,9},{9,10},{10,11},{11... | collective-permute-start | bytes 9224 | tf_op jit(solution)/shard_map/ppermute | solution.py:24
  91.7 12.5 collective-permute-start.3
  110.0 12.5 collective-permute-start.1
  146.5 12.5 collective-permute-start.1
  183.1 12.5 collective-permute-start.1
  262.0 12.5 collective-permute-start.5
  300.6 12.5 collective-permute-start.5
  339.2 12.5 collective-permute-start.5
  391.8 19.2 %collective-permute-start.27 = (f32[2,4096]{1,0:T(2,128)S(1)}, f32[2,4096]{1,0:T(2,128)S(1)}, u32[]{:S(2)}, u32[]{:S(2)}) collective-permute-start(f32[2,4096]{1,0:T(2,128)S(1)} %slice_bitcast_fusion.1), channel_id=1, source_target_pairs={{0,8},{1,9},{2,10},{3,11},{4,12},{5,13},{6,14},{7,15},{16,24},{17,... | collective-permute-start | bytes 98312 | tf_op jit(solution)/shard_map/ppermute | solution.py:35
  435.0 15.6 %collective-permute-start.30 = (f32[16,1536]{1,0:T(8,128)S(1)}, f32[16,1536]{1,0:T(8,128)S(1)}, u32[]{:S(2)}, u32[]{:S(2)}) collective-permute-start(f32[16,1536]{1,0:T(8,128)S(1)} %get-tuple-element.1107), channel_id=1, source_target_pairs={{0,1},{1,2},{2,3},{3,4},{4,5},{5,6},{6,7},{8,9},{9,10},{10,11},{11... | collective-permute-start | bytes 294920 | tf_op jit(solution)/shard_map/ppermute | solution.py:24
  682.7 12.9 collective-permute-start.9
  717.9 18.1 %collective-permute-start.38 = (f32[2,1024]{1,0:T(2,128)S(1)}, f32[2,1024]{1,0:T(2,128)S(1)}, u32[]{:S(2)}, u32[]{:S(2)}) collective-permute-start(f32[2,1024]{1,0:T(2,128)S(1)} %get-tuple-element.324), channel_id=1, source_target_pairs={{0,8},{1,9},{2,10},{3,11},{4,12},{5,13},{6,14},{7,15},{16,24},{17,... | collective-permute-start | bytes 24584 | tf_op jit(solution)/shard_map/ppermute | solution.py:35
  739.9 12.6 collective-permute-start.13
  778.6 12.5 collective-permute-start.13
  817.2 12.5 collective-permute-start.13
  855.9 12.5 collective-permute-start.13
  1200.3 13.0 collective-permute-start.17
  1219.7 12.7 collective-permute-start.19
  1235.6 18.1 %collective-permute-start.50 = (f32[2,1024]{1,0:T(2,128)S(1)}, f32[2,1024]{1,0:T(2,128)S(1)}, u32[]{:S(2)}, u32[]{:S(2)}) collective-permute-start(f32[2,1024]{1,0:T(2,128)S(1)} %get-tuple-element.326), channel_id=1, source_target_pairs={{0,8},{1,9},{2,10},{3,11},{4,12},{5,13},{6,14},{7,15},{16,24},{17,... | collective-permute-start | bytes 24584 | tf_op jit(solution)/shard_map/ppermute | solution.py:35
  1257.0 12.7 collective-permute-start.21
  1276.0 12.5 collective-permute-start.23
  1314.0 12.5 collective-permute-start.23
  1352.0 12.5 collective-permute-start.23
  1390.0 12.5 collective-permute-start.23
  (193 other events, 3459.2 us)
where the time goes:
time: 1440 us; the launch traced here: 1420 us
  waiting for transfers between devices  378 us (26%)
  starting transfers between devices  351 us (24%)
  local copies, waits for them, and re-layouts  325 us (23%)
  matrix products  293 us (20%)
  other arithmetic  68.3 us (5%)
    ppermute x59, starting transfers between devices, with_halo(): lax.ppermute(lax.slice_in_dim(block, block.shape[dim] - width, None, axis...  268 us
    ppermute x59, waiting for transfers between devices, with_halo(): lax.ppermute(lax.slice_in_dim(block, block.shape[dim] - width, None, axis...  209 us
    dot_general x59, matrix products, stencil_product(): combined = jnp.einsum('bsij,cbsj->cbi', tiles, picked, precision=highest)  162 us
    ppermute x59, waiting for transfers between devices, with_halo(): lax.ppermute(lax.slice_in_dim(block, 0, width, axis=dim), axis, backward)  137 us
    gather x10, local copies, waits for them, and re-layouts, fine_operator(): padded = with_halo(flattened[:, rim_rows], (('node', 1),), rim_width)  105 us
    dot_general x6, matrix products, restrict(): jnp.dot(flattened, mapping, precision=highest, preferred_element_type=jnp...  84.5 us
    gather x54, local copies, waits for them, and re-layouts, coarse_operator(): padded = with_halo(flattened[:, rim_rows], (('node', 1),), rim_width)  80.6 us
    ppermute x59, starting transfers between devices, with_halo(): lax.ppermute(lax.slice_in_dim(block, 0, width, axis=dim), axis, backward)  76.8 us
  transfers between devices with their start and end apart: 123, of which 108 were waited for; matrix products, arithmetic and copies ran while one was open for 4% of the time, Pallas kernels for 0%

commit v1 on v0

v1 whole, which is shorter than its diff:
```python
import functools
import jax
import jax.numpy as jnp
from jax import lax
from jax.experimental import pallas as pl
from jax.experimental.pallas import tpu as pltpu
from jax.sharding import PartitionSpec as P

SLICES = 8
ITERS = 2
LANES = 128
ROWS = 8
DT = 0.125
QUAD = ((5.0 / 96.0, 1.0 / 12.0, -1.0 / 96.0), (-1.0 / 96.0, 1.0 / 12.0, 5.0 / 96.0))

f32 = jnp.float32
bf16 = jnp.bfloat16


def take(block, lane):
    return jnp.take_along_axis(block, lane, axis=1, mode="promise_in_bounds")


def species_mask():
    return lax.broadcasted_iota(jnp.int32, (ROWS, LANES), 0) < ROWS // 2


def explicit(x, product, source):
    is_u = species_mask()
    other = pltpu.roll(x, ROWS // 2, 0)
    growth = x * other * jnp.where(is_u, other, x)
    laplacian = product - 1.5 * x
    return jnp.where(is_u, laplacian - growth, 0.5 * laplacian + growth) + source


class Level:
    def __init__(self, count, rim, cols, weights, rim_index):
        self.count = count
        self.rim = rim
        self.cols = cols
        self.weights = weights
        self.rim_index = rim_index


def rim_copies(level, ext, send, send_sem, recv_sem, node):
    rim, count = level.rim, level.count
    down = pltpu.make_async_remote_copy(
        src_ref=send.at[pl.ds(0, rim)],
        dst_ref=ext.at[pl.ds(rim + count, rim)],
        send_sem=send_sem.at[0],
        recv_sem=recv_sem.at[0],
        device_id={"node": node - 1},
        device_id_type=pl.DeviceIdType.MESH,
    )
    up = pltpu.make_async_remote_copy(
        src_ref=send.at[pl.ds(rim, rim)],
        dst_ref=ext.at[pl.ds(0, rim)],
        send_sem=send_sem.at[1],
        recv_sem=recv_sem.at[1],
        device_id={"node": node + 1},
        device_id_type=pl.DeviceIdType.MESH,
    )
    return down, up


def gather_rim(level, ext, send, side, groups):
    rim, count = level.rim, level.count
    reach = min(2 * rim, count)
    first = 0 if side == 0 else count - reach

    def body(step, carry):
        place = side * rim + step
        index = level.rim_index[place]
        lane = index & (LANES - 1)
        owner = index >> 7
        for group in range(groups):
            rows = pl.ds(group * ROWS, ROWS)
            found = take(ext[rim + first, rows, :], lane)
            for block in range(first + 1, first + reach):
                found = jnp.where(owner == block, take(ext[rim + block, rows, :], lane), found)
            send[place, rows, :] = found
        return carry

    if rim <= 3:
        for step in range(rim):
            body(step, 0)
    else:
        lax.fori_loop(0, rim, body, 0)


def operator(level, ext, send, send_sem, recv_sem, node, nodes, emit):
    groups = ext.shape[1] // ROWS
    rows = groups * ROWS
    down, up = rim_copies(level, ext, send, send_sem, recv_sem, node)
    gather_rim(level, ext, send, 0, groups)
    pl.when(node > 0)(lambda: down.start())
    gather_rim(level, ext, send, 1, groups)
    pl.when(node < nodes - 1)(lambda: up.start())
    pl.when(node < nodes - 1)(lambda: down.wait_recv())
    pl.when(node > 0)(lambda: up.wait_recv())

    def product(r):
        x = jnp.concatenate([ext[level.cols[3 * r + s]] for s in range(3)], axis=1)
        high = x.astype(bf16).astype(f32)
        both = jnp.concatenate([high, x - high], axis=0).astype(bf16)
        wide = jnp.dot(both, level.weights[r], preferred_element_type=f32)
        return wide[:rows, :LANES] + wide[:rows, LANES:] + wide[rows:, :LANES]

    if level.count <= 8:
        for r in range(level.count):
            emit(r, product(r))
    else:
        def body(r, carry):
            emit(r, product(r))
            return carry

        lax.fori_loop(0, level.count, body, 0, unroll=4)
    pl.when(node > 0)(lambda: down.wait_send())
    pl.when(node < nodes - 1)(lambda: up.wait_send())


def kernel(
    nodes,
    tms,
    cols_f,
    cols_c,
    init,
    rate,
    w_f,
    w_c,
    rim_f,
    rim_c,
    owners,
    mapping,
    out,
    ext_a,
    ext_b,
    ext_c,
    ext_d,
    ext_0,
    ext_1,
    send_a,
    send_b,
    send_c,
    send_d,
    send_0,
    send_1,
    send_sem,
    recv_sem,
    state,
    terms,
    lhs,
    coarse_rate,
    base,
    fixed,
    coarse_w,
    results,
    end_coarse,
    got_coarse,
    end_fine,
    got_fine,
    tm_send,
    tm_recv,
):
    node = lax.axis_index("node")
    tm = lax.axis_index("tm")
    per = ROWS // 2
    nb = init.shape[0]
    nbc = coarse_rate.shape[0]
    fine = Level(nb, rim_f.shape[0] // 2, cols_f, w_f, rim_f)
    coarse = Level(nbc, rim_c.shape[0] // 2, cols_c, w_c, rim_c)

    barrier = pltpu.get_barrier_semaphore()

    def greet(axis, position, size):
        for offset in (-1, 1):
            other = position + offset

            @pl.when((other >= 0) & (other < size))
            def _():
                pl.semaphore_signal(
                    barrier, inc=1, device_id={axis: other}, device_id_type=pl.DeviceIdType.MESH
                )

    greet("node", node, nodes)
    greet("tm", tm, tms)

    peers = sum(
        ((other >= 0) & (other < size)).astype(jnp.int32)
        for other, size in ((node - 1, nodes), (node + 1, nodes), (tm - 1, tms), (tm + 1, tms))
    )
    pl.semaphore_wait(barrier, peers)

    is_u = species_mask()
    row = lax.broadcasted_iota(jnp.int32, (ROWS, LANES), 0)
    slice_of = row & (per - 1)

    def restrict(pieces, write):
        count = len(pieces)

        def body(b, carry):
            lanes = pl.ds(pl.multiple_of(b * LANES, LANES), LANES)
            for g in range(count):
                x = pieces[g](b)
                high = x.astype(bf16).astype(f32)
                lhs[pl.ds(16 * g, 16), lanes] = jnp.concatenate([high, x - high], axis=0).astype(bf16)
            return carry

        lax.fori_loop(0, nb, body, 0, unroll=2)
        summed = jnp.dot(lhs[pl.ds(0, 16 * count), :], mapping[...], preferred_element_type=f32)
        for g in range(count):
            both = summed[16 * g : 16 * g + 8] + summed[16 * g + 8 : 16 * g + 16]
            for b in range(nbc):
                write(g, b, both[:, b * LANES : (b + 1) * LANES])

    def prolong(z, d):
        index = owners[d]
        lane = index & (LANES - 1)
        owner = index >> 7
        found = take(z[0], lane)
        for b in range(1, nbc):
            found = jnp.where(owner == b, take(z[b], lane), found)
        return found

    def coarse_source(b):
        return jnp.where(is_u, coarse_rate[b], 0.0)

    def fine_source(b):
        return jnp.where(is_u, rate[b], 0.0)

    def tm_copy(source, target, slot, sem):
        return pltpu.make_async_remote_copy(
            src_ref=source.at[slot],
            dst_ref=target.at[slot],
            send_sem=tm_send.at[sem],
            recv_sem=tm_recv.at[sem],
            device_id={"tm": tm + 1},
            device_id_type=pl.DeviceIdType.MESH,
        )

    def chain(number, start, has_fixed):
        copy = tm_copy(end_coarse, got_coarse, number, number)
        pl.when(tm > 0)(lambda: copy.wait_recv())
        for b in range(nbc):
            ext_0[coarse.rim + b] = jnp.where(tm == 0, start[b], got_coarse[number, b])

        def slice_body(s, carry):
            for m, (ext, send, sem, target) in enumerate(
                ((ext_0, send_0, 4, ext_1), (ext_1, send_1, 5, ext_0))
            ):
                def emit(b, product, m=m, ext=ext, target=target):
                    y = ext[coarse.rim + b]
                    value = y + DT * explicit(y, product, coarse_source(b))
                    if has_fixed:
                        value = value + fixed[m, b]
                    value = value / (1.0 + DT * coarse_rate[b])
                    results[m, b] = jnp.where(slice_of == s, value, results[m, b])
                    target[coarse.rim + b] = value if m == 0 else pltpu.roll(value, 1, 0)

                operator(coarse, ext, send, send_sem.at[sem], recv_sem.at[sem], node, nodes, emit)
            return carry

        lax.fori_loop(0, per, slice_body, 0)

        @pl.when(tm < tms - 1)
        def _():
            for b in range(nbc):
                end_coarse[number, b] = pltpu.roll(results[1, b], ROWS - (per - 1), 0)
            copy.start()

    def finish_chain(number):
        copy = tm_copy(end_coarse, got_coarse, number, number)
        pl.when(tm < tms - 1)(lambda: copy.wait_send())

    results[...] = jnp.zeros_like(results)
    for ext, rim in (
        (ext_a, fine.rim), (ext_b, fine.rim), (ext_c, fine.rim),
        (ext_d, coarse.rim), (ext_0, coarse.rim), (ext_1, coarse.rim),
    ):
        @pl.when(node == 0)
        def _(ext=ext, rim=rim):
            ext[pl.ds(0, rim)] = jnp.zeros((rim,) + ext.shape[1:], f32)

        @pl.when(node == nodes - 1)
        def _(ext=ext, rim=rim):
            ext[pl.ds(ext.shape[0] - rim, rim)] = jnp.zeros((rim,) + ext.shape[1:], f32)

    def write_base(g, b, value):
        if g == 0:
            coarse_rate[b] = value
        else:
            base[b] = value

    restrict([lambda b: rate[b], lambda b: init[b]], write_base)
    chain(0, base, False)
    finish_chain(0)

    def first_states(d, carry):
        for m in range(2):
            z = [results[m, b] - base[b] for b in range(nbc)]
            state[m, d] = init[d] + prolong(z, d)
        return carry

    lax.fori_loop(0, nb, first_states, 0)

    def iterate(it, carry):
        copy = tm_copy(end_fine, got_fine, it, 3 + it)

        @pl.when(tm < tms - 1)
        def _():
            def body(b, c):
                end_fine[it, b] = pltpu.roll(state[1, b], ROWS - (per - 1), 0)
                return c

            lax.fori_loop(0, nb, body, 0, unroll=4)
            copy.start()

        pl.when(tm > 0)(lambda: copy.wait_recv())

        def prepare(b, c):
            start = jnp.where(tm == 0, init[b], got_fine[it, b])
            last = state[1, b]
            place = fine.rim + b
            ext_a[place, 0:8] = jnp.where(slice_of == 0, start, pltpu.roll(last, 1, 0))
            ext_a[place, 8:16] = state[0, b]
            ext_a[place, 16:24] = last
            return c

        lax.fori_loop(0, nb, prepare, 0, unroll=4)

        def emit_a(r, product):
            place = fine.rim + r
            source = fine_source(r)
            decay = rate[r]
            u = [ext_a[place, 8 * m : 8 * m + 8] for m in range(3)]
            f = [explicit(u[m], product[8 * m : 8 * m + 8], source) for m in range(3)]
            g = [f[m] - decay * u[m] for m in range(3)]
            q = [sum(w * v for w, v in zip(weights, g)) for weights in QUAD]
            ext_b[place] = (u[0] + DT * decay * u[1] + q[0]) / (1.0 + DT * decay)
            terms[0, r] = g[0]
            terms[1, r] = DT * decay * u[2] + q[1] - DT * f[1]

        operator(fine, ext_a, send_a, send_sem.at[0], recv_sem.at[0], node, nodes, emit_a)
        pl.when(tm < tms - 1)(lambda: copy.wait_send())

        def emit_b(r, product):
            place = fine.rim + r
            decay = rate[r]
            v = ext_b[place]
            e = explicit(v, product, fine_source(r))
            ext_c[place] = (v + DT * e + terms[1, r]) / (1.0 + DT * decay)
            terms[1, r] = e - decay * v

        operator(fine, ext_b, send_b, send_sem.at[1], recv_sem.at[1], node, nodes, emit_b)

        def emit_c(r, product):
            v = ext_c[fine.rim + r]
            terms[2, r] = explicit(v, product, fine_source(r)) - rate[r] * v

        operator(fine, ext_c, send_c, send_sem.at[2], recv_sem.at[2], node, nodes, emit_c)

        def quad_piece(weights):
            return lambda b: sum(w * terms[m, b] for m, w in enumerate(weights))

        def write(g, b, value):
            if g < 2:
                ext_d[coarse.rim + b, 8 * g : 8 * g + 8] = value
            if g < 3:
                coarse_w[g, b] = value
            else:
                fixed[g - 3, b] = value

        restrict(
            [
                lambda b: ext_a[fine.rim + b, 0:8],
                lambda b: ext_b[fine.rim + b],
                lambda b: ext_c[fine.rim + b],
                quad_piece(QUAD[0]),
                quad_piece(QUAD[1]),
            ],
            write,
        )

        def emit_d(b, product):
            source = coarse_source(b)
            for m in range(2):
                e = explicit(coarse_w[m, b], product[8 * m : 8 * m + 8], source)
                fixed[m, b] = fixed[m, b] + DT * (coarse_rate[b] * coarse_w[m + 1, b] - e)

        operator(coarse, ext_d, send_d, send_sem.at[3], recv_sem.at[3], node, nodes, emit_d)
        chain(1 + it, coarse_w.at[0], True)
        finish_chain(1 + it)

        def new_states(d, c):
            z = [results[1, b] - coarse_w[2, b] for b in range(nbc)]
            state[1, d] = ext_c[fine.rim + d] + prolong(z, d)
            z = [results[0, b] - coarse_w[1, b] for b in range(nbc)]
            state[0, d] = ext_b[fine.rim + d] + prolong(z, d)
            return c

        lax.fori_loop(0, nb, new_states, 0)
        return carry

    lax.fori_loop(0, ITERS, iterate, 0)
    out[...] = state[1]


def spread(u, v, per):
    pieces = [u.reshape((-1, 1, LANES))] * per + [v.reshape((-1, 1, LANES))] * per
    return jnp.concatenate(pieces, axis=1)


def weight_parts(tiles):
    flipped = tiles.transpose((0, 1, 3, 2)).reshape((tiles.shape[0], -1, LANES))
    high = lax.reduce_precision(flipped, 8, 7)
    return jnp.concatenate([high.astype(bf16), (flipped - high).astype(bf16)], axis=2)


def per_device(
    nodes,
    tms,
    initial_fields,
    feed_rate,
    kill_rate,
    fine_tiles,
    fine_cols,
    fine_halo,
    coarse_tiles,
    coarse_cols,
    coarse_halo,
    children,
):
    per = SLICES // tms
    nb, nbc = fine_tiles.shape[0], coarse_tiles.shape[0]
    hb, hbc = fine_halo.shape[0] // (2 * LANES), coarse_halo.shape[0] // (2 * LANES)
    count = children.shape[0]
    init = spread(initial_fields[0], initial_fields[1], per)
    rate = spread(feed_rate, feed_rate + kill_rate, per)

    ordinal = jnp.arange(count, dtype=jnp.int32) // 4
    in_block = (children // LANES)[None, :] == jnp.arange(nb, dtype=jnp.int32)[:, None]
    left = jnp.concatenate(
        [jnp.where(in_block, ordinal // 32, 0), jnp.where(in_block, ordinal % 32, 0)], axis=0
    ).astype(bf16)
    right = (
        (children % LANES)[:, None] == jnp.arange(LANES, dtype=jnp.int32)[None, :]
    ).astype(bf16)
    halves = jnp.dot(left, right, preferred_element_type=f32).astype(jnp.int32)
    owner = halves[:nb] * 32 + halves[nb:]
    mapping = jnp.where(
        owner.reshape((-1, 1)) == jnp.arange(count // 4, dtype=jnp.int32)[None, :], 0.25, 0.0
    ).astype(bf16)

    def widen(index):
        return jnp.broadcast_to(index.reshape((-1, 1, LANES)), (index.size // LANES, ROWS, LANES))

    vmem = pl.BlockSpec(memory_space=pltpu.VMEM)
    smem = pl.BlockSpec(memory_space=pltpu.SMEM)
    fine_ext, coarse_ext = nb + 2 * hb, nbc + 2 * hbc

    def scratch(*shape):
        return pltpu.VMEM(shape + (LANES,), f32)

    result = pl.pallas_call(
        functools.partial(kernel, nodes, tms),
        out_shape=jax.ShapeDtypeStruct((nb, ROWS, LANES), f32),
        in_specs=[smem, smem] + [vmem] * 8,
        out_specs=vmem,
        scratch_shapes=[
            scratch(fine_ext, 24),
            scratch(fine_ext, 8),
            scratch(fine_ext, 8),
            scratch(coarse_ext, 16),
            scratch(coarse_ext, 8),
            scratch(coarse_ext, 8),
            scratch(2 * hb, 24),
            scratch(2 * hb, 8),
            scratch(2 * hb, 8),
            scratch(2 * hbc, 16),
            scratch(2 * hbc, 8),
            scratch(2 * hbc, 8),
            pltpu.SemaphoreType.DMA((6, 2)),
            pltpu.SemaphoreType.DMA((6, 2)),
            scratch(2, nb, ROWS),
            scratch(3, nb, ROWS),
            pltpu.VMEM((80, count), bf16),
            scratch(nbc, ROWS),
            scratch(nbc, ROWS),
            scratch(2, nbc, ROWS),
            scratch(3, nbc, ROWS),
            scratch(2, nbc, ROWS),
            scratch(1 + ITERS, nbc, ROWS),
            scratch(1 + ITERS, nbc, ROWS),
            scratch(ITERS, nb, ROWS),
            scratch(ITERS, nb, ROWS),
            pltpu.SemaphoreType.DMA((1 + 2 * ITERS,)),
            pltpu.SemaphoreType.DMA((1 + 2 * ITERS,)),
        ],
        compiler_params=pltpu.CompilerParams(
            collective_id=0, has_side_effects=True, vmem_limit_bytes=56 * 1024 * 1024
        ),
        name="pfasst",
    )(
        fine_cols.reshape((-1,)),
        coarse_cols.reshape((-1,)),
        init,
        rate,
        weight_parts(fine_tiles),
        weight_parts(coarse_tiles),
        widen(fine_halo),
        widen(coarse_halo),
        widen(owner),
        mapping,
    )
    return result.reshape((nb, 2, per, LANES)).transpose((2, 1, 0, 3)).reshape((per, 2, -1))


def solution(mesh):
    return jax.shard_map(
        functools.partial(per_device, mesh.shape["node"], mesh.shape["tm"]),
        mesh=mesh,
        in_specs=(
            P("parts", "node"),
            P("node"),
            P("node"),
            P("node", None, None, None),
            P("node", None),
            P("node"),
            P("node", None, None, None),
            P("node", None),
            P("node"),
            P("node"),
        ),
        out_specs=P("tm", "parts", "node"),
        check_vma=False,
    )
```

time: 1440 us -> 230 us (0.16); the launches traced: 1420 us -> 229 us
  waiting for transfers between devices: 378 us -> 0 us
  starting transfers between devices: 351 us -> 0 us
  local copies, waits for them, and re-layouts: 325 us -> 18.3 us
  matrix products: 293 us -> 0.75 us
  Pallas kernels: 0 us -> 195 us
  other arithmetic: 68.3 us -> 15.3 us
    ppermute x123 -> x0, waiting for transfers between devices: 378 us -> none  [the longest x59 209 us: with_halo(): lax.ppermute(lax.slice_in_dim(block, block.shape[dim] - width, None, axis...]
    ppermute x123 -> x0, starting transfers between devices: 351 us -> none  [the longest x59 268 us: with_halo(): lax.ppermute(lax.slice_in_dim(block, block.shape[dim] - width, None, axis...]
    dot_general x68 -> x1, matrix products: 293 us -> 0.75 us  [per_device(): halves = jnp.dot(left, right, preferred_element_type=f32).astype(jnp.int32)]
    gather x123 -> x0, local copies, waits for them, and re-layouts: 221 us -> none  [the longest x10 105 us: fine_operator(): padded = with_halo(flattened[:, rim_rows], (('node', 1),), rim_width)]
    pallas_call x0 -> x1, Pallas kernels: none -> 195 us  [per_device(): pl.pallas_call(functools.partial(kernel, nodes, tms), out_shape=jax.Shape...]
    div x54 -> x0, other arithmetic: 37.9 us -> none  [advance(): (previous + half_step * (terms_new - terms_old) + half_step * decay * old...]
    slice x77 -> x0, local copies, waits for them, and re-layouts: 30.2 us -> none  [the longest x65 25.1 us: with_halo(): lax.slice_in_dim(block, block.shape[dim] - width, None, axis=dim)]
    scatter x1 -> x0, local copies, waits for them, and re-layouts: 15.5 us -> none  [transfer_matrix(): position = jnp.zeros((fine_count,), jnp.int32).at[children].set(jnp.arang...]
  transfers between devices with their start and end apart: 123 -> 0, of which waited for: 108 -> 0; matrix products, arithmetic and copies ran while one was open for 4% -> 0% of each run, Pallas kernels for 0% -> 0%
where the time goes in v1:
time: 230 us; the launch traced here: 229 us
  Pallas kernels  195 us (85%)
  local copies, waits for them, and re-layouts  18.3 us (8%)
  other arithmetic  15.3 us (7%)
    pallas_call x1, Pallas kernels, per_device(): pl.pallas_call(functools.partial(kernel, nodes, tms), out_shape=jax.Shape...  195 us
    transpose x2, local copies, waits for them, and re-layouts, weight_parts(): flipped = tiles.transpose((0, 1, 3, 2)).reshape((tiles.shape[0], -1, LANES))  7.05 us
    concatenate x2, other arithmetic, weight_parts(): jnp.concatenate([high.astype(bf16), (flipped - high).astype(bf16)], axis=2)  4.83 us
    convert_element_type x2, other arithmetic, weight_parts(): high.astype(bf16)  4.8 us

profile of v1, /device:TPU:1, one launch (start us, length us, event | category | flops | bytes accessed | tf_op | source)
XLA Modules:
  0.0 229.5 jit_solution(3152111300335422711)
XLA Ops:
  0.0 0.9 copy.17
  0.9 0.7 reshape.35.cols_c
  1.5 0.7 add.19
  2.3 0.8 copy.16
  3.0 0.6 reshape.34.cols_f
  3.7 1.3 broadcast_in_dim.47.rim_c
  5.0 0.9 slice_bitcast_fusion
  5.8 0.7 add_select_fusion.4
  6.6 0.8 concatenate.16.init
  7.4 1.4 broadcast_in_dim.45.rim_f
  8.8 1.7 concatenate.17.rate
  10.5 0.1 select_convert_fusion.2
  10.6 0.8 fusion.3
  11.3 0.7 broadcast_in_dim.51.owners
  12.0 0.5 copy.19
  12.5 0.3 reduce-precision_convert_fusion.1
  12.8 1.3 pad_maximum_fusion.1.w_c
  14.1 6.6 %copy.18 = f32[32,3,128,128]{3,2,1,0:T(8,128)} copy(f32[32,3,128,128]{2,3,1,0:T(8,128)} %bitcast.23) | data formatting | bytes 12582912 | tf_op jit(solution)/shard_map/transpose | solution.py:414
  20.7 4.5 %reduce-precision_convert_fusion = (bf16[32,384,128]{2,1,0:T(8,128)(2,1)S(1)}, bf16[32,384,128]{2,1,0:T(8,128)(2,1)S(1)}) fusion(f32[32,3,128,128]{3,2,1,0:T(8,128)} %copy.18), kind=kLoop, calls=%fused_computation.3 | loop fusion | flops 6291456 | bytes 12582912 | tf_op jit(solution)/shard_map/convert_element_type | solution.py:416
  25.2 3.5 %pad_maximum_fusion.w_f = bf16[32,384,256]{2,1,0:T(8,128)(2,1)} fusion(bf16[32,384,128]{2,1,0:T(8,128)(2,1)S(1)} %get-tuple-element.6, bf16[32,384,128]{2,1,0:T(8,128)(2,1)S(1)} %get-tuple-element.5), kind=kLoop, calls=%fused_computation.5 | loop fusion | flops 12582912 | bytes 12582912 | tf_op jit(solution)/shard_map/concatenate | solution.py:416
  28.7 4.1 %select_convert_fusion.mapping = bf16[4096,1024]{1,0:T(8,128)(2,1)} fusion(s32[4096]{0:T(1024)S(1)} %fusion.19), kind=kLoop, calls=%fused_computation | loop fusion | flops 12582912 | bytes 8404992 | tf_op jit(solution)/shard_map/convert_element_type | solution.py:452
  32.9 194.9 %pfasst.1 = f32[32,8,128]{2,1,0:T(8,128)} custom-call(s32[96]{0:T(128)} %reshape.34.cols_f, s32[24]{0:T(128)} %reshape.35.cols_c, f32[32,8,128]{2,1,0:T(8,128)} %concatenate.16.init, f32[32,8,128]{2,1,0:T(8,128)} %concatenate.17.rate, bf16[32,384,256]{2,1,0:T(8,128)(2,1)} %pad_maximum_fusion.w_f, bf16[8,384,256]{2,1,0:T(8,128)(2,1)} %pad_maximum_fusion.1.w_c, ...), custom_call_target="tpu_custom_call" | custom-call | tf_op jit(solution)/shard_map/pfasst/pallas_call | solution.py:464
  227.8 0.9 copy.20
  228.7 0.7 reshape.41
  (5 shorter events, 0.0 us)
Async XLA Ops:
  0.0 12.0 %copy-start = (f32[8,3,128,128]{3,2,1,0:T(8,128)S(1)}, f32[8,3,128,128]{3,2,1,0:T(8,128)}, u32[]{:S(2)}) copy-start(f32[8,3,128,128]{3,2,1,0:T(8,128)} %param.16) | copy-start | bytes 4718596

commit v2 on v1

--- a/solution.py
+++ b/solution.py
@@ -70,7 +70,7 @@
 
     def body(step, carry):
         place = side * rim + step
-        index = level.rim_index[place]
+        index = jnp.broadcast_to(level.rim_index[pl.ds(place, 1), :], (ROWS, LANES))
         lane = index & (LANES - 1)
         owner = index >> 7
         for group in range(groups):
@@ -88,33 +88,61 @@
         lax.fori_loop(0, rim, body, 0)
 
 
-def operator(level, ext, send, send_sem, recv_sem, node, nodes, emit):
+def start_rims(level, ext, send, send_sem, recv_sem, node, nodes):
     groups = ext.shape[1] // ROWS
-    rows = groups * ROWS
     down, up = rim_copies(level, ext, send, send_sem, recv_sem, node)
     gather_rim(level, ext, send, 0, groups)
     pl.when(node > 0)(lambda: down.start())
     gather_rim(level, ext, send, 1, groups)
     pl.when(node < nodes - 1)(lambda: up.start())
+
+
+def multiply(x, weights):
+    rows = x.shape[0]
+    high = x.astype(bf16).astype(f32)
+    both = jnp.concatenate([high, x - high], axis=0).astype(bf16)
+    wide = lax.dot_general(both, weights, (((1,), (1,)), ((), ())), preferred_element_type=f32)
+    return wide[:rows, :LANES] + wide[:rows, LANES:] + wide[rows:, :LANES]
+
+
+def finish_rims(level, ext, send, send_sem, recv_sem, node, nodes, own, emit, meanwhile=None):
+    down, up = rim_copies(level, ext, send, send_sem, recv_sem, node)
+    rows = ext.shape[1]
+    batch = 8 if level.count > 8 else level.count
+
+    def own_product(r):
+        return multiply(ext[level.rim + r], level.weights[r, :, 0:LANES])
+
+    def product(r):
+        x = jnp.concatenate([ext[level.cols[r, s]] for s in range(1, 3)], axis=1)
+        return multiply(x, level.weights[r, :, LANES:])
+
+    def over_batches(function):
+        if level.count == batch:
+            function(0)
+        else:
+            def body(step, carry):
+                function(step * batch)
+                return carry
+
+            lax.fori_loop(0, level.count // batch, body, 0)
+
+    def all_own(first):
+        values = [own_product(first + i) for i in range(batch)]
+        for i in range(batch):
+            own[first + i, 0:rows] = values[i]
+
+    def all_rest(first):
+        values = [product(first + i) + own[first + i, 0:rows] for i in range(batch)]
+        for i in range(batch):
+            emit(first + i, values[i])
+
+    over_batches(all_own)
+    if meanwhile is not None:
+        meanwhile()
     pl.when(node < nodes - 1)(lambda: down.wait_recv())
     pl.when(node > 0)(lambda: up.wait_recv())
-
-    def product(r):
-        x = jnp.concatenate([ext[level.cols[3 * r + s]] for s in range(3)], axis=1)
-        high = x.astype(bf16).astype(f32)
-        both = jnp.concatenate([high, x - high], axis=0).astype(bf16)
-        wide = jnp.dot(both, level.weights[r], preferred_element_type=f32)
-        return wide[:rows, :LANES] + wide[:rows, LANES:] + wide[rows:, :LANES]
-
-    if level.count <= 8:
-        for r in range(level.count):
-            emit(r, product(r))
-    else:
-        def body(r, carry):
-            emit(r, product(r))
-            return carry
-
-        lax.fori_loop(0, level.count, body, 0, unroll=4)
+    over_batches(all_rest)
     pl.when(node > 0)(lambda: down.wait_send())
     pl.when(node < nodes - 1)(lambda: up.wait_send())
 
@@ -124,14 +152,14 @@
     tms,
     cols_f,
     cols_c,
-    init,
-    rate,
-    w_f,
-    w_c,
+    initial,
+    feed,
+    kill,
+    tiles_f,
+    tiles_c,
     rim_f,
     rim_c,
-    owners,
-    mapping,
+    children,
     out,
     ext_a,
     ext_b,
@@ -161,6 +189,20 @@
     got_fine,
     tm_send,
     tm_recv,
+    end_terms,
+    got_terms,
+    first_terms,
+    starts,
+    init,
+    rate,
+    raw_f,
+    raw_c,
+    w_f,
+    w_c,
+    mapping,
+    owners,
+    own,
+    load_sem,
 ):
     node = lax.axis_index("node")
     tm = lax.axis_index("tm")
@@ -170,6 +212,18 @@
     fine = Level(nb, rim_f.shape[0] // 2, cols_f, w_f, rim_f)
     coarse = Level(nbc, rim_c.shape[0] // 2, cols_c, w_c, rim_c)
 
+    parts = 2 * per
+    chunk = nb // parts
+
+    def load_fine(part):
+        rows = pl.ds(part * chunk, chunk)
+        return pltpu.make_async_copy(tiles_f.at[rows], raw_f.at[rows], load_sem.at[part])
+
+    load_coarse = pltpu.make_async_copy(tiles_c, raw_c, load_sem.at[parts])
+    load_coarse.start()
+    for part in range(parts):
+        load_fine(part).start()
+
     barrier = pltpu.get_barrier_semaphore()
 
     def greet(axis, position, size):
@@ -189,6 +243,59 @@
         ((other >= 0) & (other < size)).astype(jnp.int32)
         for other, size in ((node - 1, nodes), (node + 1, nodes), (tm - 1, tms), (tm + 1, tms))
     )
+
+    def split_tiles(raw, weights, r):
+        for t in range(3):
+            tile = raw[r, t]
+            high = tile.astype(bf16)
+            weights[r, 0:LANES, t * LANES : (t + 1) * LANES] = high
+            weights[r, LANES : 2 * LANES, t * LANES : (t + 1) * LANES] = (
+                tile - high.astype(f32)
+            ).astype(bf16)
+
+    def split_part(part):
+        load_fine(part).wait()
+
+        def body(i, carry):
+            split_tiles(raw_f, w_f, part * chunk + i)
+            return carry
+
+        lax.fori_loop(0, chunk, body, 0)
+
+    def place_children(c, halves):
+        line = children[pl.ds(c, 1), :]
+        owner_lane = lax.broadcasted_iota(jnp.int32, (nb, LANES), 1) >> 2
+        match = (line >> 7) == lax.broadcasted_iota(jnp.int32, (nb, LANES), 0)
+        left = jnp.concatenate(
+            [jnp.where(match, c, 0), jnp.where(match, owner_lane, 0)], axis=0
+        ).astype(f32).astype(bf16)
+        right = jnp.where(
+            (line & (LANES - 1)) == lax.broadcasted_iota(jnp.int32, (LANES, LANES), 0), 1.0, 0.0
+        ).astype(bf16)
+        return halves + lax.dot_general(
+            left, right, (((1,), (1,)), ((), ())), preferred_element_type=f32
+        )
+
+    halves = lax.fori_loop(
+        0, nb, place_children, jnp.zeros((2 * nb, LANES), f32), unroll=4
+    ).astype(jnp.int32)
+    owner_of = halves[:nb] * (LANES // 4) + halves[nb:]
+    ordinals = lax.broadcasted_iota(jnp.int32, (mapping.shape[0], LANES), 0)
+    for b in range(nb):
+        line = owner_of[b : b + 1]
+        owners[b] = jnp.broadcast_to(line, (ROWS, LANES))
+        mapping[:, b * LANES : (b + 1) * LANES] = jnp.where(ordinals == line, 0.25, 0.0).astype(bf16)
+    for b in range(nb):
+        lanes = slice(b * LANES, (b + 1) * LANES)
+        u = jnp.broadcast_to(initial[0:1, lanes], (ROWS, LANES))
+        v = jnp.broadcast_to(initial[1:2, lanes], (ROWS, LANES))
+        init[b] = jnp.where(species_mask(), u, v)
+        f = jnp.broadcast_to(feed[b : b + 1, :], (ROWS, LANES))
+        k = jnp.broadcast_to(kill[b : b + 1, :], (ROWS, LANES))
+        rate[b] = jnp.where(species_mask(), f, f + k)
+    load_coarse.wait()
+    for b in range(nbc):
+        split_tiles(raw_c, w_c, b)
     pl.semaphore_wait(barrier, peers)
 
     is_u = species_mask()
@@ -207,7 +314,12 @@
             return carry
 
         lax.fori_loop(0, nb, body, 0, unroll=2)
-        summed = jnp.dot(lhs[pl.ds(0, 16 * count), :], mapping[...], preferred_element_type=f32)
+        summed = lax.dot_general(
+            lhs[pl.ds(0, 16 * count), :],
+            mapping[...],
+            (((1,), (1,)), ((), ())),
+            preferred_element_type=f32,
+        )
         for g in range(count):
             both = summed[16 * g : 16 * g + 8] + summed[16 * g + 8 : 16 * g + 16]
             for b in range(nbc):
@@ -227,6 +339,14 @@
 
     def fine_source(b):
         return jnp.where(is_u, rate[b], 0.0)
+
+    def begin(level, ext, send, sem):
+        start_rims(level, ext, send, send_sem.at[sem], recv_sem.at[sem], node, nodes)
+
+    def finish(level, ext, send, sem, emit, meanwhile=None):
+        finish_rims(
+            level, ext, send, send_sem.at[sem], recv_sem.at[sem], node, nodes, own, emit, meanwhile
+        )
 
     def tm_copy(source, target, slot, sem):
         return pltpu.make_async_remote_copy(
@@ -257,7 +377,10 @@
                     results[m, b] = jnp.where(slice_of == s, value, results[m, b])
                     target[coarse.rim + b] = value if m == 0 else pltpu.roll(value, 1, 0)
 
-                operator(coarse, ext, send, send_sem.at[sem], recv_sem.at[sem], node, nodes, emit)
+                begin(coarse, ext, send, sem)
+                finish(
+                    coarse, ext, send, sem, emit, None if has_fixed else lambda m=m: split_part(2 * s + m)
+                )
             return carry
 
         lax.fori_loop(0, per, slice_body, 0)
@@ -292,8 +415,16 @@
             base[b] = value
 
     restrict([lambda b: rate[b], lambda b: init[b]], write_base)
+    for b in range(nb):
+        ext_b[fine.rim + b] = init[b]
+    begin(fine, ext_b, send_b, 1)
     chain(0, base, False)
     finish_chain(0)
+
+    def emit_first(r, product):
+        first_terms[r] = explicit(init[r], product, fine_source(r))
+
+    finish(fine, ext_b, send_b, 1, emit_first)
 
     def first_states(d, carry):
         for m in range(2):
@@ -315,71 +446,76 @@
             lax.fori_loop(0, nb, body, 0, unroll=4)
             copy.start()
 
-        pl.when(tm > 0)(lambda: copy.wait_recv())
-
         def prepare(b, c):
-            start = jnp.where(tm == 0, init[b], got_fine[it, b])
-            last = state[1, b]
             place = fine.rim + b
-            ext_a[place, 0:8] = jnp.where(slice_of == 0, start, pltpu.roll(last, 1, 0))
-            ext_a[place, 8:16] = state[0, b]
-            ext_a[place, 16:24] = last
+            ext_a[place, 0:8] = state[0, b]
+            ext_a[place, 8:16] = state[1, b]
             return c
 
         lax.fori_loop(0, nb, prepare, 0, unroll=4)
+        begin(fine, ext_a, send_a, 0)
+        term_copy = tm_copy(end_terms, got_terms, it, 3 + ITERS + it)
+
+        @pl.when(tm > 0)
+        def _():
+            copy.wait_recv()
+            term_copy.wait_recv()
 
         def emit_a(r, product):
-            place = fine.rim + r
             source = fine_source(r)
             decay = rate[r]
-            u = [ext_a[place, 8 * m : 8 * m + 8] for m in range(3)]
-            f = [explicit(u[m], product[8 * m : 8 * m + 8], source) for m in range(3)]
-            g = [f[m] - decay * u[m] for m in range(3)]
+            u1, u2 = state[0, r], state[1, r]
+            f1 = explicit(u1, product[0:8], source)
+            f2 = explicit(u2, product[8:16], source)
+            end_terms[it, r] = pltpu.roll(f2, ROWS - (per - 1), 0)
+            first_u = jnp.where(tm == 0, init[r], got_fine[it, r])
+            first_f = jnp.where(tm == 0, first_terms[r], got_terms[it, r])
+            u0 = jnp.where(slice_of == 0, first_u, pltpu.roll(u2, 1, 0))
+            f0 = jnp.where(slice_of == 0, first_f, pltpu.roll(f2, 1, 0))
+            g = [f0 - decay * u0, f1 - decay * u1, f2 - decay * u2]
             q = [sum(w * v for w, v in zip(weights, g)) for weights in QUAD]
-            ext_b[place] = (u[0] + DT * decay * u[1] + q[0]) / (1.0 + DT * decay)
+            ext_b[fine.rim + r] = (u0 + DT * decay * u1 + q[0]) / (1.0 + DT * decay)
+            starts[r] = u0
             terms[0, r] = g[0]
-            terms[1, r] = DT * decay * u[2] + q[1] - DT * f[1]
-
-        operator(fine, ext_a, send_a, send_sem.at[0], recv_sem.at[0], node, nodes, emit_a)
-        pl.when(tm < tms - 1)(lambda: copy.wait_send())
+            terms[1, r] = DT * decay * u2 + q[1] - DT * f1
+
+        finish(fine, ext_a, send_a, 0, emit_a)
+
+        @pl.when(tm < tms - 1)
+        def _():
+            term_copy.start()
+            copy.wait_send()
 
         def emit_b(r, product):
-            place = fine.rim + r
             decay = rate[r]
-            v = ext_b[place]
+            v = ext_b[fine.rim + r]
             e = explicit(v, product, fine_source(r))
-            ext_c[place] = (v + DT * e + terms[1, r]) / (1.0 + DT * decay)
+            ext_c[fine.rim + r] = (v + DT * e + terms[1, r]) / (1.0 + DT * decay)
             terms[1, r] = e - decay * v
 
-        operator(fine, ext_b, send_b, send_sem.at[1], recv_sem.at[1], node, nodes, emit_b)
+        begin(fine, ext_b, send_b, 1)
+        finish(fine, ext_b, send_b, 1, emit_b)
 
         def emit_c(r, product):
             v = ext_c[fine.rim + r]
             terms[2, r] = explicit(v, product, fine_source(r)) - rate[r] * v
 
-        operator(fine, ext_c, send_c, send_sem.at[2], recv_sem.at[2], node, nodes, emit_c)
-
         def quad_piece(weights):
             return lambda b: sum(w * terms[m, b] for m, w in enumerate(weights))
 
-        def write(g, b, value):
-            if g < 2:
-                ext_d[coarse.rim + b, 8 * g : 8 * g + 8] = value
-            if g < 3:
-                coarse_w[g, b] = value
+        def write_early(g, b, value):
+            ext_d[coarse.rim + b, 8 * g : 8 * g + 8] = value
+            coarse_w[g, b] = value
+
+        def write_late(g, b, value):
+            if g == 0:
+                coarse_w[2, b] = value
             else:
-                fixed[g - 3, b] = value
-
-        restrict(
-            [
-                lambda b: ext_a[fine.rim + b, 0:8],
-                lambda b: ext_b[fine.rim + b],
-                lambda b: ext_c[fine.rim + b],
-                quad_piece(QUAD[0]),
-                quad_piece(QUAD[1]),
-            ],
-            write,
-        )
+                fixed[g - 1, b] = value
+
+        def early():
+            restrict([lambda b: starts[b], lambda b: ext_b[fine.rim + b]], write_early)
+            begin(coarse, ext_d, send_d, 3)
 
         def emit_d(b, product):
             source = coarse_source(b)
@@ -387,7 +523,13 @@
                 e = explicit(coarse_w[m, b], product[8 * m : 8 * m + 8], source)
                 fixed[m, b] = fixed[m, b] + DT * (coarse_rate[b] * coarse_w[m + 1, b] - e)
 
-        operator(coarse, ext_d, send_d, send_sem.at[3], recv_sem.at[3], node, nodes, emit_d)
+        begin(fine, ext_c, send_c, 2)
+        finish(fine, ext_c, send_c, 2, emit_c, early)
+        restrict(
+            [lambda b: ext_c[fine.rim + b], quad_piece(QUAD[0]), quad_piece(QUAD[1])], write_late
+        )
+        finish(coarse, ext_d, send_d, 3, emit_d)
+        pl.when(tm < tms - 1)(lambda: term_copy.wait_send())
         chain(1 + it, coarse_w.at[0], True)
         finish_chain(1 + it)
 
@@ -402,18 +544,8 @@
         return carry
 
     lax.fori_loop(0, ITERS, iterate, 0)
-    out[...] = state[1]
-
-
-def spread(u, v, per):
-    pieces = [u.reshape((-1, 1, LANES))] * per + [v.reshape((-1, 1, LANES))] * per
-    return jnp.concatenate(pieces, axis=1)
-
-
-def weight_parts(tiles):
-    flipped = tiles.transpose((0, 1, 3, 2)).reshape((tiles.shape[0], -1, LANES))
-    high = lax.reduce_precision(flipped, 8, 7)
-    return jnp.concatenate([high.astype(bf16), (flipped - high).astype(bf16)], axis=2)
+    for b in range(nb):
+        out[:, b * LANES : (b + 1) * LANES] = state[1, b]
 
 
 def per_device(
@@ -434,26 +566,6 @@
     nb, nbc = fine_tiles.shape[0], coarse_tiles.shape[0]
     hb, hbc = fine_halo.shape[0] // (2 * LANES), coarse_halo.shape[0] // (2 * LANES)
     count = children.shape[0]
-    init = spread(initial_fields[0], initial_fields[1], per)
-    rate = spread(feed_rate, feed_rate + kill_rate, per)
-
-    ordinal = jnp.arange(count, dtype=jnp.int32) // 4
-    in_block = (children // LANES)[None, :] == jnp.arange(nb, dtype=jnp.int32)[:, None]
-    left = jnp.concatenate(
-        [jnp.where(in_block, ordinal // 32, 0), jnp.where(in_block, ordinal % 32, 0)], axis=0
-    ).astype(bf16)
-    right = (
-        (children % LANES)[:, None] == jnp.arange(LANES, dtype=jnp.int32)[None, :]
-    ).astype(bf16)
-    halves = jnp.dot(left, right, preferred_element_type=f32).astype(jnp.int32)
-    owner = halves[:nb] * 32 + halves[nb:]
-    mapping = jnp.where(
-        owner.reshape((-1, 1)) == jnp.arange(count // 4, dtype=jnp.int32)[None, :], 0.25, 0.0
-    ).astype(bf16)
-
-    def widen(index):
-        return jnp.broadcast_to(index.reshape((-1, 1, LANES)), (index.size // LANES, ROWS, LANES))
-
     vmem = pl.BlockSpec(memory_space=pltpu.VMEM)
     smem = pl.BlockSpec(memory_space=pltpu.SMEM)
     fine_ext, coarse_ext = nb + 2 * hb, nbc + 2 * hbc
@@ -461,19 +573,20 @@
     def scratch(*shape):
         return pltpu.VMEM(shape + (LANES,), f32)
 
+    anywhere = pl.BlockSpec(memory_space=pl.ANY)
     result = pl.pallas_call(
         functools.partial(kernel, nodes, tms),
-        out_shape=jax.ShapeDtypeStruct((nb, ROWS, LANES), f32),
-        in_specs=[smem, smem] + [vmem] * 8,
+        out_shape=jax.ShapeDtypeStruct((ROWS, count), f32),
+        in_specs=[smem, smem, vmem, vmem, vmem, anywhere, anywhere, vmem, vmem, vmem],
         out_specs=vmem,
         scratch_shapes=[
-            scratch(fine_ext, 24),
+            scratch(fine_ext, 16),
             scratch(fine_ext, 8),
             scratch(fine_ext, 8),
             scratch(coarse_ext, 16),
             scratch(coarse_ext, 8),
             scratch(coarse_ext, 8),
-            scratch(2 * hb, 24),
+            scratch(2 * hb, 16),
             scratch(2 * hb, 8),
             scratch(2 * hb, 8),
             scratch(2 * hbc, 16),
@@ -493,26 +606,40 @@
             scratch(1 + ITERS, nbc, ROWS),
             scratch(ITERS, nb, ROWS),
             scratch(ITERS, nb, ROWS),
-            pltpu.SemaphoreType.DMA((1 + 2 * ITERS,)),
-            pltpu.SemaphoreType.DMA((1 + 2 * ITERS,)),
+            pltpu.SemaphoreType.DMA((1 + 3 * ITERS,)),
+            pltpu.SemaphoreType.DMA((1 + 3 * ITERS,)),
+            scratch(ITERS, nb, ROWS),
+            scratch(ITERS, nb, ROWS),
+            scratch(nb, ROWS),
+            scratch(nb, ROWS),
+            scratch(nb, ROWS),
+            scratch(nb, ROWS),
+            scratch(nb, 3, LANES),
+            scratch(nbc, 3, LANES),
+            pltpu.VMEM((nb, 2 * LANES, 3 * LANES), bf16),
+            pltpu.VMEM((nbc, 2 * LANES, 3 * LANES), bf16),
+            pltpu.VMEM((count // 4, count), bf16),
+            pltpu.VMEM((nb, ROWS, LANES), jnp.int32),
+            scratch(nb, 2 * ROWS),
+            pltpu.SemaphoreType.DMA((2 * per + 1,)),
         ],
         compiler_params=pltpu.CompilerParams(
             collective_id=0, has_side_effects=True, vmem_limit_bytes=56 * 1024 * 1024
         ),
         name="pfasst",
     )(
-        fine_cols.reshape((-1,)),
-        coarse_cols.reshape((-1,)),
-        init,
-        rate,
-        weight_parts(fine_tiles),
-        weight_parts(coarse_tiles),
-        widen(fine_halo),
-        widen(coarse_halo),
-        widen(owner),
-        mapping,
+        fine_cols,
+        coarse_cols,
+        initial_fields,
+        feed_rate.reshape((nb, LANES)),
+        kill_rate.reshape((nb, LANES)),
+        fine_tiles,
+        coarse_tiles,
+        fine_halo.reshape((-1, LANES)),
+        coarse_halo.reshape((-1, LANES)),
+        children.reshape((nb, LANES)),
     )
-    return result.reshape((nb, 2, per, LANES)).transpose((2, 1, 0, 3)).reshape((per, 2, -1))
+    return result.reshape((2, per, count)).transpose((1, 0, 2))
 
 
 def solution(mesh):

time: 230 us -> 199 us (0.87)
  other arithmetic: 15.3 us -> 0 us
  local copies, waits for them, and re-layouts: 18.3 us -> 4.41 us
    convert_element_type x3 -> x0, other arithmetic: 8.94 us -> none  [the longest x2 4.8 us: weight_parts(): high.astype(bf16)]
    transpose x3 -> x0, local copies, waits for them, and re-layouts: 7.98 us -> none  [the longest x2 7.05 us: weight_parts(): flipped = tiles.transpose((0, 1, 3, 2)).reshape((tiles.shape[0], -1, LANES))]
    concatenate x2 -> x0, other arithmetic: 4.83 us -> none  [weight_parts(): jnp.concatenate([high.astype(bf16), (flipped - high).astype(bf16)], axis=2)]
    broadcast_in_dim x3 -> x0, local copies, waits for them, and re-layouts: 3.3 us -> none  [widen(): jnp.broadcast_to(index.reshape((-1, 1, LANES)), (index.size // LANES, ROW...]
    concatenate x2 -> x0, local copies, waits for them, and re-layouts: 2.54 us -> none  [spread(): return jnp.concatenate(pieces, axis=1)]
where the time goes in v2:
time: 199 us
  Pallas kernels  194 us (97%)
  local copies, waits for them, and re-layouts  4.41 us (2%)
    pallas_call x1, Pallas kernels, per_device(): pl.pallas_call(functools.partial(kernel, nodes, tms), out_shape=jax.Shape...  194 us

profile of v2, /device:TPU:1, one launch (start us, length us, event | category | flops | bytes accessed | tf_op | source)
XLA Modules:
  0.0 198.7 jit_solution(1842453291399125552)
XLA Ops:
  0.0 1.3 copy.12.cols_c
  1.3 1.4 copy.11.cols_f
  2.7 194.3 %pfasst.1 = f32[8,4096]{1,0:T(8,128)} custom-call(s32[32,3]{1,0:T(8,128)} %copy.11.cols_f, s32[8,3]{1,0:T(8,128)} %copy.12.cols_c, f32[2,4096]{1,0:T(2,128)} %initial.1, f32[32,128]{1,0:T(8,128)} %bitcast.8, f32[32,128]{1,0:T(8,128)} %bitcast.9, f32[32,3,128,128]{3,2,1,0:T(8,128)} %tiles_f.1, f32[8,3,128,128]{3,2,1,0:T(8,128)} %tiles_c.1, ...), custom_call_target="tpu_custom_call" | custom-call | tf_op jit(solution)/shard_map/pfasst/pallas_call | solution.py:577
  197.0 0.9 reshape.23
  197.9 0.8 copy.15

commit v3 on v2

--- a/solution.py
+++ b/solution.py
@@ -101,7 +101,7 @@
     rows = x.shape[0]
     high = x.astype(bf16).astype(f32)
     both = jnp.concatenate([high, x - high], axis=0).astype(bf16)
-    wide = lax.dot_general(both, weights, (((1,), (1,)), ((), ())), preferred_element_type=f32)
+    wide = jnp.dot(both, weights, preferred_element_type=f32)
     return wide[:rows, :LANES] + wide[:rows, LANES:] + wide[rows:, :LANES]
 
 
@@ -111,11 +111,11 @@
     batch = 8 if level.count > 8 else level.count
 
     def own_product(r):
-        return multiply(ext[level.rim + r], level.weights[r, :, 0:LANES])
+        return multiply(ext[level.rim + r], level.weights[r, 0:LANES, :])
 
     def product(r):
         x = jnp.concatenate([ext[level.cols[r, s]] for s in range(1, 3)], axis=1)
-        return multiply(x, level.weights[r, :, LANES:])
+        return multiply(x, level.weights[r, LANES:, :])
 
     def over_batches(function):
         if level.count == batch:
@@ -143,6 +143,10 @@
     pl.when(node < nodes - 1)(lambda: down.wait_recv())
     pl.when(node > 0)(lambda: up.wait_recv())
     over_batches(all_rest)
+
+
+def settle_rims(level, ext, send, send_sem, recv_sem, node, nodes):
+    down, up = rim_copies(level, ext, send, send_sem, recv_sem, node)
     pl.when(node > 0)(lambda: down.wait_send())
     pl.when(node < nodes - 1)(lambda: up.wait_send())
 
@@ -179,6 +183,7 @@
     terms,
     lhs,
     coarse_rate,
+    coarse_scale,
     base,
     fixed,
     coarse_w,
@@ -246,10 +251,10 @@
 
     def split_tiles(raw, weights, r):
         for t in range(3):
-            tile = raw[r, t]
+            tile = raw[r, t].T
             high = tile.astype(bf16)
-            weights[r, 0:LANES, t * LANES : (t + 1) * LANES] = high
-            weights[r, LANES : 2 * LANES, t * LANES : (t + 1) * LANES] = (
+            weights[r, t * LANES : (t + 1) * LANES, 0:LANES] = high
+            weights[r, t * LANES : (t + 1) * LANES, LANES : 2 * LANES] = (
                 tile - high.astype(f32)
             ).astype(bf16)
 
@@ -276,15 +281,17 @@
             left, right, (((1,), (1,)), ((), ())), preferred_element_type=f32
         )
 
-    halves = lax.fori_loop(
-        0, nb, place_children, jnp.zeros((2 * nb, LANES), f32), unroll=4
-    ).astype(jnp.int32)
+    halves = lax.fori_loop(0, nb, place_children, jnp.zeros((2 * nb, LANES), f32), unroll=4)
     owner_of = halves[:nb] * (LANES // 4) + halves[nb:]
-    ordinals = lax.broadcasted_iota(jnp.int32, (mapping.shape[0], LANES), 0)
+    ordinals = lax.broadcasted_iota(jnp.int32, (LANES, LANES), 1).astype(f32)
     for b in range(nb):
         line = owner_of[b : b + 1]
-        owners[b] = jnp.broadcast_to(line, (ROWS, LANES))
-        mapping[:, b * LANES : (b + 1) * LANES] = jnp.where(ordinals == line, 0.25, 0.0).astype(bf16)
+        owners[b] = jnp.broadcast_to(line, (ROWS, LANES)).astype(jnp.int32)
+        column = jnp.broadcast_to(line, (LANES, LANES)).T
+        for n in range(nbc):
+            mapping[b * LANES : (b + 1) * LANES, n * LANES : (n + 1) * LANES] = jnp.where(
+                column == ordinals + float(n * LANES), 0.25, 0.0
+            ).astype(bf16)
     for b in range(nb):
         lanes = slice(b * LANES, (b + 1) * LANES)
         u = jnp.broadcast_to(initial[0:1, lanes], (ROWS, LANES))
@@ -314,12 +321,7 @@
             return carry
 
         lax.fori_loop(0, nb, body, 0, unroll=2)
-        summed = lax.dot_general(
-            lhs[pl.ds(0, 16 * count), :],
-            mapping[...],
-            (((1,), (1,)), ((), ())),
-            preferred_element_type=f32,
-        )
+        summed = jnp.dot(lhs[pl.ds(0, 16 * count), :], mapping[...], preferred_element_type=f32)
         for g in range(count):
             both = summed[16 * g : 16 * g + 8] + summed[16 * g + 8 : 16 * g + 16]
             for b in range(nbc):
@@ -347,6 +349,9 @@
         finish_rims(
             level, ext, send, send_sem.at[sem], recv_sem.at[sem], node, nodes, own, emit, meanwhile
         )
+
+    def settle(level, ext, send, sem):
+        settle_rims(level, ext, send, send_sem.at[sem], recv_sem.at[sem], node, nodes)
 
     def tm_copy(source, target, slot, sem):
         return pltpu.make_async_remote_copy(
@@ -373,7 +378,7 @@
                     value = y + DT * explicit(y, product, coarse_source(b))
                     if has_fixed:
                         value = value + fixed[m, b]
-                    value = value / (1.0 + DT * coarse_rate[b])
+                    value = value * coarse_scale[b]
                     results[m, b] = jnp.where(slice_of == s, value, results[m, b])
                     target[coarse.rim + b] = value if m == 0 else pltpu.roll(value, 1, 0)
 
@@ -381,6 +386,10 @@
                 finish(
                     coarse, ext, send, sem, emit, None if has_fixed else lambda m=m: split_part(2 * s + m)
                 )
+                if m == 1:
+                    settle(coarse, ext_0, send_0, 4)
+                else:
+                    pl.when(s > 0)(lambda: settle(coarse, ext_1, send_1, 5))
             return carry
 
         lax.fori_loop(0, per, slice_body, 0)
@@ -390,6 +399,8 @@
             for b in range(nbc):
                 end_coarse[number, b] = pltpu.roll(results[1, b], ROWS - (per - 1), 0)
             copy.start()
+
+        settle(coarse, ext_1, send_1, 5)
 
     def finish_chain(number):
         copy = tm_copy(end_coarse, got_coarse, number, number)
@@ -411,6 +422,7 @@
     def write_base(g, b, value):
         if g == 0:
             coarse_rate[b] = value
+            coarse_scale[b] = 1.0 / (1.0 + DT * value)
         else:
             base[b] = value
 
@@ -425,6 +437,7 @@
         first_terms[r] = explicit(init[r], product, fine_source(r))
 
     finish(fine, ext_b, send_b, 1, emit_first)
+    settle(fine, ext_b, send_b, 1)
 
     def first_states(d, carry):
         for m in range(2):
@@ -529,6 +542,10 @@
             [lambda b: ext_c[fine.rim + b], quad_piece(QUAD[0]), quad_piece(QUAD[1])], write_late
         )
         finish(coarse, ext_d, send_d, 3, emit_d)
+        settle(fine, ext_a, send_a, 0)
+        settle(fine, ext_b, send_b, 1)
+        settle(fine, ext_c, send_c, 2)
+        settle(coarse, ext_d, send_d, 3)
         pl.when(tm < tms - 1)(lambda: term_copy.wait_send())
         chain(1 + it, coarse_w.at[0], True)
         finish_chain(1 + it)
@@ -599,6 +616,7 @@
             pltpu.VMEM((80, count), bf16),
             scratch(nbc, ROWS),
             scratch(nbc, ROWS),
+            scratch(nbc, ROWS),
             scratch(2, nbc, ROWS),
             scratch(3, nbc, ROWS),
             scratch(2, nbc, ROWS),
@@ -616,9 +634,9 @@
             scratch(nb, ROWS),
             scratch(nb, 3, LANES),
             scratch(nbc, 3, LANES),
-            pltpu.VMEM((nb, 2 * LANES, 3 * LANES), bf16),
-            pltpu.VMEM((nbc, 2 * LANES, 3 * LANES), bf16),
-            pltpu.VMEM((count // 4, count), bf16),
+            pltpu.VMEM((nb, 3 * LANES, 2 * LANES), bf16),
+            pltpu.VMEM((nbc, 3 * LANES, 2 * LANES), bf16),
+            pltpu.VMEM((count, count // 4), bf16),
             pltpu.VMEM((nb, ROWS, LANES), jnp.int32),
             scratch(nb, 2 * ROWS),
             pltpu.SemaphoreType.DMA((2 * per + 1,)),

time: 199 us -> 186 us (0.935)
  Pallas kernels: 194 us -> 180 us
    pallas_call x1, Pallas kernels: 194 us -> 180 us  [per_device(): pl.pallas_call(functools.partial(kernel, nodes, tms), out_shape=jax.Shape...]
where the time goes in v3:
time: 186 us; the launch traced here: 185 us
  Pallas kernels  180 us (97%)
  local copies, waits for them, and re-layouts  4.41 us (2%)
    pallas_call x1, Pallas kernels, per_device(): pl.pallas_call(functools.partial(kernel, nodes, tms), out_shape=jax.Shape...  180 us

profile of v3, /device:TPU:1, one launch (start us, length us, event | category | flops | bytes accessed | tf_op | source)
XLA Modules:
  0.0 184.6 jit_solution(17980088614931188778)
XLA Ops:
  0.0 1.3 copy.12.cols_c
  1.3 1.4 copy.11.cols_f
  2.7 180.1 %pfasst.1 = f32[8,4096]{1,0:T(8,128)} custom-call(s32[32,3]{1,0:T(8,128)} %copy.11.cols_f, s32[8,3]{1,0:T(8,128)} %copy.12.cols_c, f32[2,4096]{1,0:T(2,128)} %initial.1, f32[32,128]{1,0:T(8,128)} %bitcast.8, f32[32,128]{1,0:T(8,128)} %bitcast.9, f32[32,3,128,128]{3,2,1,0:T(8,128)} %tiles_f.1, f32[8,3,128,128]{3,2,1,0:T(8,128)} %tiles_c.1, ...), custom_call_target="tpu_custom_call" | custom-call | tf_op jit(solution)/shard_map/pfasst/pallas_call | solution.py:594
  182.9 0.9 reshape.23
  183.8 0.8 copy.15
